TPU v7x, 128 devices: a whole 4x4x4 slice. The times are simulated.
128 devices in a mesh: rep: 16 (over z, x_lo, core), shard: 8 (over y, x_hi).
Axes of the slice: x: 4 (x_hi: 2, x_lo: 2; x = x_hi * 2 + x_lo), y: 4, z: 4, core: 2. Of those that a mesh axis runs over, the one named last changes fastest.
Arguments:
- plan: int32 [8192], P('shard'), may hold values from 0 to 1
- local_params: bfloat16 [2, 16, 8192, 2048], P(None, 'rep', 'shard'), may hold values from -6 to 6
- master: float32 [2, 8192, 2048], P(None, 'shard', 'rep'), may hold values from -6 to 6
- momentum: float32 [2, 8192, 2048], P(None, 'shard', 'rep'), may hold values from -6 to 6
- inner_weight: bfloat16 [16, 8192, 512], P('rep', 'shard'), may hold values from -0.0625 to 0.0625
- activations: bfloat16 [16, 2048, 8192], P('rep', 'shard'), may hold values from -6 to 6
- out_grad: bfloat16 [16, 2048, 512], P('rep', 'shard'), may hold values from -6 to 6
Outputs:
- new_params: bfloat16 [8192, 2048], P('shard')
- new_master: float32 [8192, 2048], P('shard', 'rep')
- new_momentum: float32 [8192, 2048], P('shard', 'rep')
- keys_out: bfloat16 [16, 2048, 512], P('rep', 'shard')
- input_grad: bfloat16 [16, 2048, 8192], P('rep', 'shard')
- weight_grad: bfloat16 [16, 8192, 512], P('rep', 'shard')
All inputs are finite; a program needn't handle non-finite values.
Results may differ from a plain program's by a relative error of at most 0.017.
Values may be sent and summed in bfloat16 or wider, within the bound.
A program may use at most 128 MiB of HBM per device.

v0:
```python
import jax
import jax.numpy as jnp
from jax import lax
from jax.sharding import PartitionSpec as P

OUTER_LR = 0.7
OUTER_MU = 0.9


def body(plan, local_params, master, momentum, inner_weight, activations, out_grad):
    local = local_params[0, 0]
    master_now = master[0]
    moment_now = momentum[0]
    picked = (plan == 1)[:, None]
    local = jnp.where(picked, local_params[1, 0], local)
    master_now = jnp.where(picked, master[1], master_now)
    moment_now = jnp.where(picked, momentum[1], moment_now)
    replicas = lax.axis_size("rep")
    total = lax.psum_scatter(
        local.astype(jnp.float32).astype(jnp.bfloat16), "rep", scatter_dimension=1, tiled=True
    ).astype(jnp.float32)
    outer_grad = master_now - total / replicas
    new_momentum = OUTER_MU * moment_now + outer_grad
    new_master = master_now - OUTER_LR * (outer_grad + OUTER_MU * new_momentum)
    new_params = lax.all_gather(new_master.astype(jnp.bfloat16), "rep", axis=1, tiled=True)
    weight = inner_weight[0]
    inputs = activations[0]
    cotangent = out_grad[0]
    piece = lax.all_gather(weight, "shard", axis=0, tiled=True)
    keys_acc = jnp.dot(inputs, piece, preferred_element_type=jnp.float32)
    back_part = lax.dot_general(
        cotangent, piece, (((1,), (1,)), ((), ())), preferred_element_type=jnp.float32
    )
    grad_term = lax.dot_general(
        inputs, cotangent, (((0,), (0,)), ((), ())), preferred_element_type=jnp.float32
    )
    grad_sum = lax.psum_scatter(
        grad_term.astype(jnp.bfloat16), "shard", scatter_dimension=0, tiled=True
    )
    keys_out = keys_acc.astype(jnp.bfloat16)[None]
    input_grad = back_part.astype(jnp.bfloat16)[None]
    weight_grad = grad_sum[None]
    return (new_params, new_master, new_momentum, keys_out, input_grad, weight_grad)


def solution(mesh):
    placed = (
        P("shard"),
        P(None, "rep", "shard", None),
        P(None, "shard", "rep"),
        P(None, "shard", "rep"),
        P("rep", "shard", None),
        P("rep", "shard", None),
        P("rep", "shard", None),
    )
    return jax.shard_map(
        body,
        mesh=mesh,
        in_specs=placed,
        out_specs=(
            P("shard", None),
            P("shard", "rep"),
            P("shard", "rep"),
            P("rep", "shard", None),
            P("rep", "shard", None),
            P("rep", "shard", None),
        ),
        check_vma=False,
    )
```

profile of v0, /device:TPU:0, one launch (start us, length us, event | category | flops | bytes accessed | tf_op | source)
XLA Modules:
  0.0 324.6 jit_solution(16097084172832570921)
XLA Ops:
  8.0 0.0 copy-start
  8.0 0.0 reduce-scatter.7.cloned.1.call-start
  8.1 0.7 broadcast_compare_fusion
  8.8 5.2 %bitcast_select_fusion = bf16[1024,2048]{1,0:T(8,128)(2,1)} fusion(bf16[2,1,1024,2048]{3,2,1,0:T(8,128)(2,1)} %param.8, pred[1024]{0:T(1024)(128)(4,1)S(1)} %broadcast_compare_fusion), kind=kLoop, calls=%fused_computation.8 | loop fusion | flops 2097152 | bytes 12583936 | tf_op jit(solution)/shard_map/jit(_where)/select_n | solution.py:15
  14.0 6.4 %copy.13 = bf16[1024,2048]{0,1:T(8,128)(2,1)} copy(bf16[1024,2048]{1,0:T(8,128)(2,1)} %bitcast_select_fusion) | data formatting | bytes 8388608
  20.4 0.0 reduce-scatter.7.cloned.1.call-update
  20.4 0.0 all-gather.6.cloned.1.call-start
  20.5 0.5 all-gather.6.cloned.1.call-update
  21.0 0.0 all-gather.4.cloned.1.call-start
  21.1 126.4 %reduce-scatter.7.cloned.1.call-done = bf16[128,1024]{1,0:T(8,128)(2,1)} async-done(((bf16[2048,1024]{1,0:T(8,128)(2,1)}), bf16[128,1024]{1,0:T(8,128)(2,1)}) %reduce-scatter.7.cloned.1.call-update) | async-done | bytes 262160
  147.5 1.1 copy.14
  148.6 0.0 copy-done.3
  148.6 1.3 fusion.20
  150.0 0.0 all-gather.4.cloned.1.call-update
  150.0 0.0 reduce-scatter.5.cloned.1.call-start
  150.1 7.8 %convolution_convert_fusion = bf16[8192,512]{1,0:T(8,128)(2,1)} fusion(bf16[1,256,8192]{2,1,0:T(8,128)(2,1)} %param.12, bf16[1,256,512]{2,1,0:T(8,128)(2,1)S(1)} %copy-done), kind=kOutput, calls=%fused_computation | convolution fusion | flops 2151677952 | bytes 12845056 | tf_op jit(solution)/shard_map/dot_general | solution.py:34
  157.9 0.0 reduce-scatter.5.cloned.1.call-update
  157.9 0.0 all-gather.6.cloned.1.call-done
  157.9 0.0 copy-start.2
  158.0 8.0 %fusion = bf16[1,256,8192]{2,1,0:T(8,128)(2,1)} fusion(bf16[1,8192,512]{2,1,0:T(8,128)(2,1)} %all-gather.6.cloned.1.call-done, bf16[1,256,512]{2,1,0:T(8,128)(2,1)S(1)} %copy-done), kind=kOutput, calls=%fused_computation.2 | convolution fusion | flops 2149580800 | bytes 12845056 | tf_op jit(solution)/shard_map/dot_general | solution.py:31
  165.9 3.0 fusion.11
  169.0 25.8 %all-gather.4.cloned.1.call-done = bf16[1024,2048]{1,0:T(8,128)(2,1)} async-done(((bf16[1024,128]{1,0:T(8,128)(2,1)}), bf16[1024,2048]{1,0:T(8,128)(2,1)}) %all-gather.4.cloned.1.call-update) | async-done | bytes 4194320 | tf_op jit(solution)/shard_map/all_gather | solution.py:25
  194.8 117.4 %reduce-scatter.5.cloned.1.call-done = bf16[1024,512]{1,0:T(8,128)(2,1)} async-done(((bf16[8192,512]{1,0:T(8,128)(2,1)}), bf16[1024,512]{1,0:T(8,128)(2,1)}) %reduce-scatter.5.cloned.1.call-update) | async-done | bytes 1048592 | tf_op jit(solution)/shard_map/reduce_scatter | solution.py:37
  312.3 4.8 %copy.16 = bf16[1024,2048]{1,0:T(8,128)(2,1)} copy(bf16[1024,2048]{1,0:T(8,128)(2,1)} %all-gather.4.cloned.1.call-done) | data formatting | bytes 8388608
  (7 shorter events, 0.0 us)
Async XLA Ops:
  8.0 142.1 %copy-start = (bf16[1,256,512]{2,1,0:T(8,128)(2,1)S(1)}, bf16[1,256,512]{2,1,0:T(8,128)(2,1)}, u32[]{:S(2)}) copy-start(bf16[1,256,512]{2,1,0:T(8,128)(2,1)} %param.13) | copy-start | bytes 786436
  8.0 139.5 %reduce-scatter.7.cloned.1.call-start = ((), (), s32[]{:S(2)}) async-start(), calls=%async_computation.5 | async-start | bytes 4456448
  20.4 128.2 %copy-start.3 = (f32[2,1024,128]{2,1,0:T(8,128)S(1)}, f32[2,1024,128]{2,1,0:T(8,128)}, u32[]{:S(2)}) copy-start(f32[2,1024,128]{2,1,0:T(8,128)} %param.9) | copy-start | bytes 3145732
  20.4 128.2 %copy-start.4 = (f32[2,1024,128]{2,1,0:T(8,128)S(1)}, f32[2,1024,128]{2,1,0:T(8,128)}, u32[]{:S(2)}) copy-start(f32[2,1024,128]{2,1,0:T(8,128)} %param.10) | copy-start | bytes 3145732
  20.4 137.5 %all-gather.6.cloned.1.call-start = ((), (), s32[]{:S(2)}) async-start(), calls=%async_computation.4 | async-start | bytes 9437184 | tf_op jit(solution)/shard_map/all_gather | solution.py:29
  21.0 173.8 %all-gather.4.cloned.1.call-start = ((), (), s32[]{:S(2)}) async-start(), calls=%async_computation.2 | async-start | bytes 4456448 | tf_op jit(solution)/shard_map/all_gather | solution.py:25
  150.0 162.3 %reduce-scatter.5.cloned.1.call-start = ((), (), s32[]{:S(2)}) async-start(), calls=%async_computation.3 | async-start | bytes 9437184 | tf_op jit(solution)/shard_map/reduce_scatter | solution.py:37
  157.9 8.0 %copy-start.1 = (bf16[1,8192,512]{2,1,0:T(8,128)(2,1)S(1)}, bf16[1,8192,512]{2,1,0:T(8,128)(2,1)}, u32[]{:S(2)}) copy-start(bf16[1,8192,512]{2,1,0:T(8,128)(2,1)} %all-gather.6.cloned.1.call-done) | copy-start | bytes 25165828
  157.9 8.0 %copy-start.2 = (bf16[1,256,8192]{2,1,0:T(8,128)(2,1)S(1)}, bf16[1,256,8192]{2,1,0:T(8,128)(2,1)}, u32[]{:S(2)}) copy-start(bf16[1,256,8192]{2,1,0:T(8,128)(2,1)} %param.12) | copy-start | bytes 12582916
Sparse Core Ops, SparseCore 0:
  20.5 126.9 reduce-scatter.6
Sparse Core Ops, SparseCore 1:
  23.2 111.4 all-gather.5
  150.1 44.7 all-gather.3
  199.1 113.1 reduce-scatter.4
where the time goes:
time: 325 us
  waiting for transfers between devices  270 us (83%)
  matrix products  18.8 us (6%)
  between operations  15.7 us (5%)
  local copies, waits for them, and re-layouts  12.3 us (4%)
  other arithmetic  7.28 us (2%)
    unnamed x5, waiting for transfers between devices  127 us
    reduce_scatter x1, waiting for transfers between devices, body(): lax.psum_scatter(grad_term.astype(jnp.bfloat16), 'shard', scatter_dimensi...  117 us
    all_gather x1, waiting for transfers between devices, body(): lax.all_gather(new_master.astype(jnp.bfloat16), 'rep', axis=1, tiled=True)  25.8 us
    unnamed x13, local copies, waits for them, and re-layouts  12.3 us
    dot_general x1, matrix products, body(): lax.dot_general(cotangent, piece, (((1,), (1,)), ((), ())), preferred_ele...  7.99 us
    dot_general x1, matrix products, body(): lax.dot_general(inputs, cotangent, (((0,), (0,)), ((), ())), preferred_el...  7.81 us
  transfers between devices with their start and end apart: 4, of which 3 were waited for; matrix products, arithmetic and copies ran while one was open for 7% of the time, Pallas kernels for 0%

commit v1 on v0

v1 whole, which is shorter than its diff:
```python
import jax
import jax.numpy as jnp
from jax import lax
from jax.experimental import pallas as pl
from jax.experimental.pallas import tpu as pltpu
from jax.sharding import PartitionSpec as P

OUTER_LR = 0.7
OUTER_MU = 0.9
BF = jnp.bfloat16
F32 = jnp.float32
D, KVC, INNER, TOK = 8192, 2048, 512, 256
BLK = 1024
QR = 256
HALF = 512
QS = range(4)
HS = range(2)

KEYS = (
    [("g1", w, q) for w in "SUD" for q in QS]
    + [("g2", w, q) for w, qs in (("U", (0, 1)), ("D", (2, 3))) for q in qs]
    + [("g3", w, q) for w in "UD" for q in QS]
    + [("g4", q) for q in QS]
    + [("ra", w, q) for w in "UD" for q in QS]
    + [("x1", q) for q in QS]
    + [("rb", w, i) for w in "UD" for i in HS]
    + [("rc", w, q) for w in "UD" for q in QS]
    + [("x2", q) for q in QS]
    + [("c1", h) for h in HS]
    + [("zb", w) for w in "UD"]
    + [("zc", w, h) for w in "UD" for h in HS]
    + [("xr", h) for h in HS]
    + [("xp", h) for h in HS]
    + [("zp", w, h) for w in "UD" for h in HS]
    + [("zf", w) for w in "UD"]
    + [("c2", k, h) for k in range(4) for h in HS]
)
SEM = {key: i for i, key in enumerate(KEYS)}
LOCAL = (
    ["og", "plan", "w", "mast", "mom", "np", "nm", "nmo", "keys", "wg"]
    + [("act", j) for j in range(8)]
    + [("lp", k) for k in QS]
    + [("ig", j) for j in range(8)]
)
LSEM = {key: i for i, key in enumerate(LOCAL)}


def kernel(
    plan_h, lp_h, mast_h, mom_h, w_h, act_h, og_h,
    np_o, nm_o, nmo_o, keys_o, ig_o, wg_o,
    plan_v, pick, lpb, sel, cr, zb, zc, xr, npv, mast, mom, nm, nmo,
    act, og, wg, tt, ra, rx1, rb, rc, rx2, ig, acc, keysv,
    ss, rs, ls,
):
    rep, shard = lax.axis_index("rep"), lax.axis_index("shard")
    z, xl, c = rep // 4, (rep // 2) % 2, rep % 2
    y, xh = shard // 2, shard % 2
    yu, yd, yo = (y + 1) % 4, (y + 3) % 4, (y + 2) % 4
    zu, zd, zo = (z + 1) % 4, (z + 3) % 4, (z + 2) % 4
    me, sib = shard, y * 2 + 1 - xh
    bu, bd, bo = yu * 2 + xh, yd * 2 + xh, yo * 2 + xh
    bus, bds, bos = yu * 2 + 1 - xh, yd * 2 + 1 - xh, yo * 2 + 1 - xh
    to = {
        "U": (rep, bu), "D": (rep, bd), "S": (rep, sib),
        "X": (z * 4 + (1 - xl) * 2 + c, shard), "C": (z * 4 + xl * 2 + 1 - c, shard),
        "ZU": (zu * 4 + xl * 2 + c, shard), "ZD": (zd * 4 + xl * 2 + c, shard),
    }
    started = []

    def send(src, dst, key, way):
        copy = pltpu.make_async_remote_copy(
            src_ref=src, dst_ref=dst, send_sem=ss.at[SEM[key]], recv_sem=rs.at[SEM[key]],
            device_id=to[way], device_id_type=pl.DeviceIdType.MESH,
        )
        copy.start()
        started.append(copy)

    def arrived(dst, key, way):
        pltpu.make_async_remote_copy(
            src_ref=dst, dst_ref=dst, send_sem=ss.at[SEM[key]], recv_sem=rs.at[SEM[key]],
            device_id=to[way], device_id_type=pl.DeviceIdType.MESH,
        ).wait_recv()

    def fetch(src, dst, key):
        copy = pltpu.make_async_copy(src, dst, ls.at[LSEM[key]])
        copy.start()
        return copy

    def rows(block, q=0, n=QR):
        return pl.ds(pl.multiple_of(block * BLK + q * QR, QR), n)

    def cols(block, i=0, n=BLK):
        return pl.ds(pl.multiple_of(block * BLK + i, QR), n)

    f_og = fetch(og_h.at[0], og, "og")
    order = [bus, bds, bos, bu, bd, bo, sib, me]
    f_act = [fetch(act_h.at[0, :, cols(j)], act.at[:, cols(j)], ("act", i)) for i, j in enumerate(order)]
    f_plan = fetch(plan_h, plan_v, "plan")
    f_lp = [
        fetch(lp_h.at[:, 0, pl.ds(k * QR, QR)], lpb.at[k % 2], ("lp", k)) for k in (0, 1)
    ]
    f_w = fetch(w_h.at[0], wg.at[rows(me, 0, BLK)], "w")
    f_mast = fetch(mast_h, mast, "mast")
    f_mom = fetch(mom_h, mom, "mom")

    barrier = pltpu.get_barrier_semaphore()
    for device in to.values():
        pl.semaphore_signal(barrier, inc=1, device_id=device, device_id_type=pl.DeviceIdType.MESH)
    pl.semaphore_wait(barrier, len(to))

    for q in QS:
        for w in "SUD":
            send(w_h.at[0, pl.ds(q * QR, QR)], wg.at[rows(me, q)], ("g1", w, q), w)

    f_og.wait()

    def term(block):
        def sub(i, _):
            a = act[:, cols(block, i * QR, QR)]
            t = lax.dot_general(a, og[...], (((0,), (0,)), ((), ())), preferred_element_type=F32)
            tt[rows(block, i), :] = t.astype(BF)
            return 0

        lax.fori_loop(0, 4, sub, 0)

    for i, block in enumerate(order):
        f_act[i].wait()
        term(block)
        if i == 0:
            for q in QS:
                send(tt.at[rows(block, q)], ra.at[0, pl.ds(q * QR, QR)], ("ra", "U", q), "U")
        if i == 1:
            for q in QS:
                send(tt.at[rows(block, q)], ra.at[1, pl.ds(q * QR, QR)], ("ra", "D", q), "D")
        if i == 2:
            for q in QS:
                send(tt.at[rows(block, q)], rx1.at[pl.ds(q * QR, QR)], ("x1", q), "S")
        if i == 3:
            for q in (0, 1):
                send(tt.at[rows(block, q)], rc.at[0, pl.ds(q * QR, QR)], ("rc", "U", q), "U")
        if i == 4:
            for q in (2, 3):
                send(tt.at[rows(block, q)], rc.at[1, pl.ds(q * QR, QR)], ("rc", "D", q), "D")

    f_plan.wait()
    for g in range(8):
        line = plan_v[pl.ds(g, 1), :].astype(F32)
        pick[pl.ds(g * 128, 128), :] = jnp.broadcast_to(line, (128, 128)).T

    for k in QS:
        f_lp[k].wait()

        def choose(i, _, k=k):
            r = pl.multiple_of(i * 64, 64)
            mask = pick[pl.ds(k * QR + r, 64), :] == 1.0
            for b in range(16):
                a0 = lpb[k % 2, 0, pl.ds(r, 64), b * 128 : (b + 1) * 128].astype(F32)
                a1 = lpb[k % 2, 1, pl.ds(r, 64), b * 128 : (b + 1) * 128].astype(F32)
                sel[b % 2, k // 2, b // 4, (b // 2) % 2, pl.ds((k % 2) * QR + r, 64), :] = jnp.where(
                    mask, a1, a0
                ).astype(BF)
            return 0

        lax.fori_loop(0, 4, choose, 0)
        if k < 2:
            f_lp.append(
                fetch(lp_h.at[:, 0, pl.ds((k + 2) * QR, QR)], lpb.at[k % 2], ("lp", k + 2))
            )
        if k % 2 == 1:
            send(sel.at[1 - c, k // 2], cr.at[k // 2], ("c1", k // 2), "C")

    acc[...] = jnp.zeros_like(acc)
    out_copies = []

    def layer(block, n):
        def sub(i, _):
            at = cols(block, i * HALF, HALF)
            w = wg[at, :]
            acc[...] += jnp.dot(act[:, at], w, preferred_element_type=F32)
            ig[:, at] = lax.dot_general(
                og[...], w, (((1,), (1,)), ((), ())), preferred_element_type=F32
            ).astype(BF)
            return 0

        lax.fori_loop(0, 2, sub, 0)
        out_copies.append(fetch(ig.at[:, cols(block)], ig_o.at[0, :, cols(block)], ("ig", n)))

    def add_into(dst, dst_row, *sources):
        def sub(i, _):
            at = pl.ds(pl.multiple_of(dst_row + i * 64, 64), 64)
            total = dst[at, :].astype(F32)
            for ref, row in sources:
                total = total + ref[pl.ds(row + i * 64, 64), :].astype(F32)
            dst[at, :] = total.astype(BF)
            return 0

        lax.fori_loop(0, QR // 64, sub, 0)

    f_w.wait()
    layer(me, 0)

    def core_sum(zz, h):
        def sub(i, _):
            at = pl.ds(pl.multiple_of(i * 128, 128), 128)
            for l in HS:
                sel[c, h, zz, l, at, :] = (
                    sel[c, h, zz, l, at, :].astype(F32) + cr[h, zz, l, at, :].astype(F32)
                ).astype(BF)
            return 0

        lax.fori_loop(0, 4, sub, 0)

    for h in HS:
        arrived(cr.at[h], ("c1", h), "C")
    core_sum(zo, 0)
    send(sel.at[c, 0, zo], zb.at[1], ("zb", "D"), "ZD")
    core_sum(zo, 1)
    send(sel.at[c, 1, zo], zb.at[0], ("zb", "U"), "ZU")
    core_sum(zu, 0)
    send(sel.at[c, 0, zu], zc.at[0, 0], ("zc", "U", 0), "ZU")
    core_sum(zd, 1)
    send(sel.at[c, 1, zd], zc.at[1, 1], ("zc", "D", 1), "ZD")
    core_sum(zu, 1)
    core_sum(zd, 0)
    core_sum(z, 0)
    core_sum(z, 1)

    for q in (0, 1):
        arrived(wg.at[rows(bd, q)], ("g1", "U", q), "D")
        send(wg.at[rows(bd, q)], wg.at[rows(bd, q)], ("g2", "U", q), "U")
        arrived(wg.at[rows(bu, q)], ("g1", "D", q), "U")
    for q in (2, 3):
        arrived(wg.at[rows(bu, q)], ("g1", "D", q), "U")
        send(wg.at[rows(bu, q)], wg.at[rows(bu, q)], ("g2", "D", q), "D")
        arrived(wg.at[rows(bd, q)], ("g1", "U", q), "D")

    def z_add(dst, h, zz, way):
        def sub(i, _):
            at = pl.ds(pl.multiple_of(i * 128, 128), 128)
            for l in HS:
                sel[c, h, zz, l, at, :] = (
                    sel[c, h, zz, l, at, :].astype(F32) + zb[way, l, at, :].astype(F32)
                ).astype(BF)
            return 0

        lax.fori_loop(0, 4, sub, 0)

    arrived(zb.at[0], ("zb", "U"), "ZD")
    z_add(sel, 1, zu, 0)
    send(sel.at[c, 1, zu], zc.at[0, 1], ("zc", "U", 1), "ZU")
    arrived(zb.at[1], ("zb", "D"), "ZU")
    z_add(sel, 0, zd, 1)
    send(sel.at[c, 0, zd], zc.at[1, 0], ("zc", "D", 0), "ZD")

    layer(bd, 1)
    layer(bu, 2)
    for q in QS:
        arrived(wg.at[rows(sib, q)], ("g1", "S", q), "S")
    layer(sib, 3)

    for h in HS:
        arrived(zc.at[0, h], ("zc", "U", h), "ZD")
        arrived(zc.at[1, h], ("zc", "D", h), "ZU")

        def z_sum(i, _, h=h):
            at = pl.ds(pl.multiple_of(i * 128, 128), 128)
            sel[c, h, z, 1 - xl, at, :] = (
                sel[c, h, z, 1 - xl, at, :].astype(F32)
                + zc[0, h, 1 - xl, at, :].astype(F32)
                + zc[1, h, 1 - xl, at, :].astype(F32)
            ).astype(BF)
            return 0

        lax.fori_loop(0, 4, z_sum, 0)
        send(sel.at[c, h, z, 1 - xl], xr.at[h], ("xr", h), "X")

    for q in (0, 2, 1, 3):
        arrived(rx1.at[pl.ds(q * QR, QR)], ("x1", q), "S")
        add_into(tt, bo * BLK + q * QR, (rx1, q * QR))
        way = "D" if q < 2 else "U"
        side = 1 if q < 2 else 0
        send(tt.at[rows(bo, q)], rb.at[side, pl.ds((q % 2) * QR, QR)], ("rb", way, q % 2), way)

    for q in (0, 1):
        for w in "UD":
            send(wg.at[rows(sib, q)], wg.at[rows(sib, q)], ("g3", w, q), w)

    for q in QS:
        arrived(ra.at[0, pl.ds(q * QR, QR)], ("ra", "U", q), "D")
        arrived(ra.at[1, pl.ds(q * QR, QR)], ("ra", "D", q), "U")
        add_into(tt, sib * BLK + q * QR, (ra.at[0], q * QR), (ra.at[1], q * QR))
        send(tt.at[rows(sib, q)], rx2.at[pl.ds(q * QR, QR)], ("x2", q), "S")

    f_mast.wait()
    f_mom.wait()
    for h in HS:
        arrived(xr.at[h], ("xr", h), "X")

        def update(i, _, h=h):
            at = pl.ds(pl.multiple_of(i * 64, 64), 64)
            to_row = pl.ds(pl.multiple_of(h * HALF + i * 64, 64), 64)
            total = (
                sel[c, h, z, xl, at, :].astype(F32)
                + zc[0, h, xl, at, :].astype(F32)
                + zc[1, h, xl, at, :].astype(F32)
                + xr[h, at, :].astype(F32)
            )
            mask = pick[to_row, :] == 1.0
            master_now = jnp.where(mask, mast[1, to_row, :], mast[0, to_row, :])
            moment_now = jnp.where(mask, mom[1, to_row, :], mom[0, to_row, :])
            outer_grad = master_now - total / 16
            new_momentum = OUTER_MU * moment_now + outer_grad
            new_master = master_now - OUTER_LR * (outer_grad + OUTER_MU * new_momentum)
            nmo[to_row, :] = new_momentum
            nm[to_row, :] = new_master
            npv[c, h, z, xl, at, :] = new_master.astype(BF)
            return 0

        lax.fori_loop(0, 8, update, 0)
        send(npv.at[c, h, z, xl], npv.at[c, h, z, xl], ("xp", h), "X")
    out_copies.append(fetch(nm, nm_o, "nm"))
    out_copies.append(fetch(nmo, nmo_o, "nmo"))

    for q in QS:
        way, back = ("U", "D") if q < 2 else ("D", "U")
        arrived(wg.at[rows(bo, q)], ("g2", way, q), back)
        send(wg.at[rows(bo, q)], wg.at[rows(bo, q)], ("g4", q), "S")

    for h in HS:
        arrived(npv.at[c, h, z, 1 - xl], ("xp", h), "X")
        for w in "UD":
            send(npv.at[c, h, z], npv.at[c, h, z], ("zp", w, h), "Z" + w)
        send(npv.at[c, h, z], npv.at[c, h, z], ("c2", 0, h), "C")

    layer(bo, 4)

    for i in HS:
        arrived(rb.at[0, pl.ds(i * QR, QR)], ("rb", "U", i), "D")
        add_into(tt, bu * BLK + (2 + i) * QR, (rb.at[0], i * QR))
        q = 2 + i
        send(tt.at[rows(bu, q)], rc.at[0, pl.ds(q * QR, QR)], ("rc", "U", q), "U")
        arrived(rb.at[1, pl.ds(i * QR, QR)], ("rb", "D", i), "U")
        add_into(tt, bd * BLK + i * QR, (rb.at[1], i * QR))
        send(tt.at[rows(bd, i)], rc.at[1, pl.ds(i * QR, QR)], ("rc", "D", i), "D")

    for q in (2, 3):
        for w in "UD":
            send(wg.at[rows(sib, q)], wg.at[rows(sib, q)], ("g3", w, q), w)

    for h in HS:
        arrived(npv.at[c, h, zd], ("zp", "U", h), "ZD")
        if h == 0:
            send(npv.at[c, 0, zd], npv.at[c, 0, zd], ("zf", "U"), "ZU")
        send(npv.at[c, h, zd], npv.at[c, h, zd], ("c2", 1, h), "C")
        arrived(npv.at[c, h, zu], ("zp", "D", h), "ZU")
        if h == 1:
            send(npv.at[c, 1, zu], npv.at[c, 1, zu], ("zf", "D"), "ZD")
        send(npv.at[c, h, zu], npv.at[c, h, zu], ("c2", 2, h), "C")
    arrived(npv.at[c, 0, zo], ("zf", "U"), "ZD")
    send(npv.at[c, 0, zo], npv.at[c, 0, zo], ("c2", 3, 0), "C")
    arrived(npv.at[c, 1, zo], ("zf", "D"), "ZU")
    send(npv.at[c, 1, zo], npv.at[c, 1, zo], ("c2", 3, 1), "C")

    for h in HS:
        for k, zz in enumerate((z, zd, zu, zo)):
            arrived(npv.at[1 - c, h, zz], ("c2", k, h), "C")
    for b in range(16):
        for h in HS:
            pltpu.make_async_copy(
                npv.at[b % 2, h, b // 4, (b // 2) % 2],
                np_o.at[pl.ds(h * HALF, HALF), pl.ds(b * 128, 128)],
                ls.at[LSEM["np"]],
            ).start()

    for q in QS:
        arrived(wg.at[rows(bos, q)], ("g4", q), "S")
    layer(bos, 5)

    for q in QS:
        arrived(rx2.at[pl.ds(q * QR, QR)], ("x2", q), "S")
    for q in QS:
        arrived(rc.at[0, pl.ds(q * QR, QR)], ("rc", "U", q), "D")
        arrived(rc.at[1, pl.ds(q * QR, QR)], ("rc", "D", q), "U")
        add_into(tt, me * BLK + q * QR, (rc.at[0], q * QR), (rc.at[1], q * QR), (rx2, q * QR))
    out_copies.append(fetch(tt.at[rows(me, 0, BLK)], wg_o.at[0], "wg"))

    for n, (block, way, back) in enumerate(((bds, "U", "D"), (bus, "D", "U"))):
        for q in QS:
            arrived(wg.at[rows(block, q)], ("g3", way, q), back)
        layer(block, 6 + n)
    keysv[...] = acc[...].astype(BF)
    out_copies.append(fetch(keysv, keys_o.at[0], "keys"))

    for copy in started:
        copy.wait_send()
    for copy in out_copies:
        copy.wait()
    pltpu.make_async_copy(np_o, np_o, ls.at[LSEM["np"]]).wait()


def body(plan, local_params, master, momentum, inner_weight, activations, out_grad):
    vm = pltpu.VMEM
    any_spec = pl.BlockSpec(memory_space=pl.ANY)
    return pl.pallas_call(
        kernel,
        out_shape=(
            jax.ShapeDtypeStruct((BLK, KVC), BF),
            jax.ShapeDtypeStruct((BLK, 128), F32),
            jax.ShapeDtypeStruct((BLK, 128), F32),
            jax.ShapeDtypeStruct((1, TOK, INNER), BF),
            jax.ShapeDtypeStruct((1, TOK, D), BF),
            jax.ShapeDtypeStruct((1, BLK, INNER), BF),
        ),
        in_specs=[any_spec] * 7,
        out_specs=[any_spec] * 6,
        scratch_shapes=[
            vm((8, 128), jnp.int32),
            vm((BLK, 128), F32),
            vm((2, 2, QR, KVC), BF),
            vm((2, 2, 4, 2, HALF, 128), BF),
            vm((2, 4, 2, HALF, 128), BF),
            vm((2, 2, HALF, 128), BF),
            vm((2, 2, 2, HALF, 128), BF),
            vm((2, HALF, 128), BF),
            vm((2, 2, 4, 2, HALF, 128), BF),
            vm((2, BLK, 128), F32),
            vm((2, BLK, 128), F32),
            vm((BLK, 128), F32),
            vm((BLK, 128), F32),
            vm((TOK, D), BF),
            vm((TOK, INNER), BF),
            vm((D, INNER), BF),
            vm((D, INNER), BF),
            vm((2, BLK, INNER), BF),
            vm((BLK, INNER), BF),
            vm((2, HALF, INNER), BF),
            vm((2, BLK, INNER), BF),
            vm((BLK, INNER), BF),
            vm((TOK, D), BF),
            vm((TOK, INNER), F32),
            vm((TOK, INNER), BF),
            pltpu.SemaphoreType.DMA((len(KEYS),)),
            pltpu.SemaphoreType.DMA((len(KEYS),)),
            pltpu.SemaphoreType.DMA((len(LOCAL),)),
        ],
        compiler_params=pltpu.CompilerParams(
            collective_id=0, has_side_effects=True, vmem_limit_bytes=60 << 20
        ),
        cost_estimate=pl.CostEstimate(
            flops=6 * TOK * D * INNER, bytes_accessed=26 << 20, transcendentals=0
        ),
        name="sync_and_layer",
    )(plan.reshape(8, 128), local_params, master, momentum, inner_weight, activations, out_grad)


def solution(mesh):
    placed = (
        P("shard"),
        P(None, "rep", "shard", None),
        P(None, "shard", "rep"),
        P(None, "shard", "rep"),
        P("rep", "shard", None),
        P("rep", "shard", None),
        P("rep", "shard", None),
    )
    return jax.shard_map(
        body,
        mesh=mesh,
        in_specs=placed,
        out_specs=(
            P("shard", None),
            P("shard", "rep"),
            P("shard", "rep"),
            P("rep", "shard", None),
            P("rep", "shard", None),
            P("rep", "shard", None),
        ),
        check_vma=False,
    )
```

time: 325 us -> 136 us (0.42)
  waiting for transfers between devices: 270 us -> 0 us
  Pallas kernels: 0 us -> 125 us
  matrix products: 18.8 us -> 0 us
  between operations: 15.7 us -> 0.68 us
  other arithmetic: 7.28 us -> 0 us
    unnamed x5 -> x0, waiting for transfers between devices: 127 us -> none
    pallas_call x0 -> x1, Pallas kernels: none -> 125 us  [body(): pl.pallas_call(kernel, out_shape=(jax.ShapeDtypeStruct((BLK, KVC), BF), j...]
    reduce_scatter x1 -> x0, waiting for transfers between devices: 117 us -> none  [body(): lax.psum_scatter(grad_term.astype(jnp.bfloat16), 'shard', scatter_dimensi...]
    all_gather x2 -> x0, waiting for transfers between devices: 25.9 us -> none  [the longest x1 25.8 us: body(): lax.all_gather(new_master.astype(jnp.bfloat16), 'rep', axis=1, tiled=True)]
    dot_general x3 -> x0, matrix products: 18.8 us -> none  [the longest x1 7.99 us: body(): lax.dot_general(cotangent, piece, (((1,), (1,)), ((), ())), preferred_ele...]
    select_n x1 -> x0, other arithmetic: 5.22 us -> none  [body(): local = jnp.where(picked, local_params[1, 0], local)]
    unnamed x13 -> x16, local copies, waits for them, and re-layouts: 12.3 us -> 10.2 us
  transfers between devices with their start and end apart: 4 -> 0, of which waited for: 3 -> 0; matrix products, arithmetic and copies ran while one was open for 7% -> 0% of each run, Pallas kernels for 0% -> 0%
where the time goes in v1:
time: 136 us
  Pallas kernels  125 us (92%)
  local copies, waits for them, and re-layouts  10.2 us (7%)
    pallas_call x1, Pallas kernels, body(): pl.pallas_call(kernel, out_shape=(jax.ShapeDtypeStruct((BLK, KVC), BF), j...  125 us
    unnamed x16, local copies, waits for them, and re-layouts  10.2 us

profile of v1, /device:TPU:0, one launch (start us, length us, event | category | flops | bytes accessed | tf_op | source)
XLA Modules:
  0.0 135.7 jit_solution(52309674453571517)
XLA Ops:
  0.6 124.8 %sync_and_layer.1 = (bf16[1024,2048]{1,0:T(8,128)(2,1)}, f32[1024,128]{1,0:T(8,128)}, f32[1024,128]{1,0:T(8,128)}, bf16[1,256,512]{2,1,0:T(8,128)(2,1)}, bf16[1,...) custom-call(s32[8,128]{1,0:T(8,128)} %bitcast.1, bf16[2,1,1024,2048]{3,2,1,0:T(8,128)(2,1)} %lp_h.1, ...), custom_call_target="tpu_custom_call" | custom-call | flops 6442450944 | bytes 27262976 | tf_op jit(solution)/shard_map/sync_and_layer/pallas_call | solution.py:404
  125.4 0.0 copy-start.3
  125.4 0.0 copy-start.2
  125.5 0.0 copy-start.4
  125.5 0.0 copy-start
  125.5 4.9 %copy.19 = bf16[1024,2048]{1,0:T(8,128)(2,1)} copy(bf16[1024,2048]{1,0:T(8,128)(2,1)} %get-tuple-element.12) | data formatting | bytes 8388608
  130.4 0.0 copy-done.3
  130.4 0.8 copy.20
  131.2 0.0 copy-done.2
  131.2 0.8 copy.21
  132.0 0.0 copy-done.4
  132.0 0.7 copy.22
  132.7 0.0 copy-done
  132.7 0.0 copy-start.1
  132.7 2.0 %copy.23 = bf16[1,256,8192]{2,1,0:T(8,128)(2,1)} copy(bf16[1,256,8192]{2,1,0:T(8,128)(2,1)S(1)} %copy-done) | data formatting | bytes 8388608
  134.7 0.0 copy-done.1
  134.7 1.0 copy.24
Async XLA Ops:
  125.4 5.0 %copy-start.3 = (f32[1024,128]{1,0:T(8,128)S(1)}, f32[1024,128]{1,0:T(8,128)}, u32[]{:S(2)}) copy-start(f32[1024,128]{1,0:T(8,128)} %get-tuple-element.13) | copy-start | bytes 1572868
  125.4 5.8 %copy-start.2 = (f32[1024,128]{1,0:T(8,128)S(1)}, f32[1024,128]{1,0:T(8,128)}, u32[]{:S(2)}) copy-start(f32[1024,128]{1,0:T(8,128)} %get-tuple-element.14) | copy-start | bytes 1572868
  125.5 6.6 %copy-start.4 = (bf16[1,256,512]{2,1,0:T(8,128)(2,1)S(1)}, bf16[1,256,512]{2,1,0:T(8,128)(2,1)}, u32[]{:S(2)}) copy-start(bf16[1,256,512]{2,1,0:T(8,128)(2,1)} %get-tuple-element.15) | copy-start | bytes 786436
  125.5 7.2 %copy-start = (bf16[1,256,8192]{2,1,0:T(8,128)(2,1)S(1)}, bf16[1,256,8192]{2,1,0:T(8,128)(2,1)}, u32[]{:S(2)}) copy-start(bf16[1,256,8192]{2,1,0:T(8,128)(2,1)} %get-tuple-element.16) | copy-start | bytes 12582916
  132.7 2.0 %copy-start.1 = (bf16[1,1024,512]{2,1,0:T(8,128)(2,1)S(1)}, bf16[1,1024,512]{2,1,0:T(8,128)(2,1)}, u32[]{:S(2)}) copy-start(bf16[1,1024,512]{2,1,0:T(8,128)(2,1)} %get-tuple-element.17) | copy-start | bytes 3145732

commit v2 on v1

--- a/solution.py
+++ b/solution.py
@@ -17,15 +17,15 @@
 HS = range(2)
 
 KEYS = (
-    [("g1", w, q) for w in "SUD" for q in QS]
+    [("og",)]
+    + [("ax", k) for k in range(4)]
+    + [("g1", w, q) for w in "SUD" for q in QS]
     + [("g2", w, q) for w, qs in (("U", (0, 1)), ("D", (2, 3))) for q in qs]
     + [("g3", w, q) for w in "UD" for q in QS]
-    + [("g4", q) for q in QS]
-    + [("ra", w, q) for w in "UD" for q in QS]
-    + [("x1", q) for q in QS]
+    + [("g4", q) for q in (1, 2)]
+    + [("g5", w) for w in "UD"]
     + [("rb", w, i) for w in "UD" for i in HS]
     + [("rc", w, q) for w in "UD" for q in QS]
-    + [("x2", q) for q in QS]
     + [("c1", h) for h in HS]
     + [("zb", w) for w in "UD"]
     + [("zc", w, h) for w in "UD" for h in HS]
@@ -37,19 +37,18 @@
 )
 SEM = {key: i for i, key in enumerate(KEYS)}
 LOCAL = (
-    ["og", "plan", "w", "mast", "mom", "np", "nm", "nmo", "keys", "wg"]
+    ["og", "plan", "w", "mast", "mom", "np"]
     + [("act", j) for j in range(8)]
     + [("lp", k) for k in QS]
-    + [("ig", j) for j in range(8)]
 )
 LSEM = {key: i for i, key in enumerate(LOCAL)}
 
 
 def kernel(
     plan_h, lp_h, mast_h, mom_h, w_h, act_h, og_h,
-    np_o, nm_o, nmo_o, keys_o, ig_o, wg_o,
-    plan_v, pick, lpb, sel, cr, zb, zc, xr, npv, mast, mom, nm, nmo,
-    act, og, wg, tt, ra, rx1, rb, rc, rx2, ig, acc, keysv,
+    np_o, nm, nmo, keys_o, ig, wg_o,
+    plan_v, pick, lpb, sel, cr, zb, zc, xr, npv, mast, mom,
+    act, og, acts, ogs, wg, tt, rb, rc, acc,
     ss, rs, ls,
 ):
     rep, shard = lax.axis_index("rep"), lax.axis_index("shard")
@@ -92,14 +91,14 @@
     def cols(block, i=0, n=BLK):
         return pl.ds(pl.multiple_of(block * BLK + i, QR), n)
 
-    f_og = fetch(og_h.at[0], og, "og")
-    order = [bus, bds, bos, bu, bd, bo, sib, me]
-    f_act = [fetch(act_h.at[0, :, cols(j)], act.at[:, cols(j)], ("act", i)) for i, j in enumerate(order)]
     f_plan = fetch(plan_h, plan_v, "plan")
     f_lp = [
         fetch(lp_h.at[:, 0, pl.ds(k * QR, QR)], lpb.at[k % 2], ("lp", k)) for k in (0, 1)
     ]
+    f_og = fetch(og_h.at[0], og, "og")
     f_w = fetch(w_h.at[0], wg.at[rows(me, 0, BLK)], "w")
+    order = [me, bo, bu, bd, bus, bds, bos, sib]
+    f_act = [fetch(act_h.at[0, :, cols(j)], act.at[:, cols(j)], ("act", i)) for i, j in enumerate(order)]
     f_mast = fetch(mast_h, mast, "mast")
     f_mom = fetch(mom_h, mom, "mom")
 
@@ -108,39 +107,20 @@
         pl.semaphore_signal(barrier, inc=1, device_id=device, device_id_type=pl.DeviceIdType.MESH)
     pl.semaphore_wait(barrier, len(to))
 
+    def tokens_to_sibling(k):
+        yy = (yo, yu, yd, y)[k]
+        send(act_h.at[0, :, cols(yy * 2 + 1 - xh)], acts.at[yy], ("ax", k), "S")
+
     for q in QS:
-        for w in "SUD":
+        for w in "UD":
             send(w_h.at[0, pl.ds(q * QR, QR)], wg.at[rows(me, q)], ("g1", w, q), w)
-
-    f_og.wait()
-
-    def term(block):
-        def sub(i, _):
-            a = act[:, cols(block, i * QR, QR)]
-            t = lax.dot_general(a, og[...], (((0,), (0,)), ((), ())), preferred_element_type=F32)
-            tt[rows(block, i), :] = t.astype(BF)
-            return 0
-
-        lax.fori_loop(0, 4, sub, 0)
-
-    for i, block in enumerate(order):
-        f_act[i].wait()
-        term(block)
-        if i == 0:
-            for q in QS:
-                send(tt.at[rows(block, q)], ra.at[0, pl.ds(q * QR, QR)], ("ra", "U", q), "U")
-        if i == 1:
-            for q in QS:
-                send(tt.at[rows(block, q)], ra.at[1, pl.ds(q * QR, QR)], ("ra", "D", q), "D")
-        if i == 2:
-            for q in QS:
-                send(tt.at[rows(block, q)], rx1.at[pl.ds(q * QR, QR)], ("x1", q), "S")
-        if i == 3:
-            for q in (0, 1):
-                send(tt.at[rows(block, q)], rc.at[0, pl.ds(q * QR, QR)], ("rc", "U", q), "U")
-        if i == 4:
-            for q in (2, 3):
-                send(tt.at[rows(block, q)], rc.at[1, pl.ds(q * QR, QR)], ("rc", "D", q), "D")
+        if q == 0:
+            send(og_h.at[0], ogs, ("og",), "S")
+            tokens_to_sibling(0)
+    tokens_to_sibling(1)
+
+    def weight_to_sibling(q):
+        send(w_h.at[0, pl.ds(q * QR, QR)], wg.at[rows(me, q)], ("g1", "S", q), "S")
 
     f_plan.wait()
     for g in range(8):
@@ -169,21 +149,37 @@
         if k % 2 == 1:
             send(sel.at[1 - c, k // 2], cr.at[k // 2], ("c1", k // 2), "C")
 
+    f_og.wait()
     acc[...] = jnp.zeros_like(acc)
-    out_copies = []
-
-    def layer(block, n):
+
+    def layer(block, q0=0, n=4):
         def sub(i, _):
-            at = cols(block, i * HALF, HALF)
+            at = cols(block, (q0 + i) * QR, QR)
             w = wg[at, :]
             acc[...] += jnp.dot(act[:, at], w, preferred_element_type=F32)
-            ig[:, at] = lax.dot_general(
+            ig[0, :, at] = lax.dot_general(
                 og[...], w, (((1,), (1,)), ((), ())), preferred_element_type=F32
             ).astype(BF)
             return 0
 
-        lax.fori_loop(0, 2, sub, 0)
-        out_copies.append(fetch(ig.at[:, cols(block)], ig_o.at[0, :, cols(block)], ("ig", n)))
+        lax.fori_loop(0, n, sub, 0)
+
+    def term(k):
+        yy = (yo, yu, yd, y)[k]
+        arrived(acts.at[yy], ("ax", k), "S")
+        if k == 0:
+            tokens_to_sibling(2)
+
+        def sub(i, _):
+            at = pl.ds(pl.multiple_of(i * QR, QR), QR)
+            over_tokens = (((0,), (0,)), ((), ()))
+            t = lax.dot_general(
+                act[:, cols(yy * 2 + xh, i * QR, QR)], og[...], over_tokens, preferred_element_type=F32
+            ) + lax.dot_general(acts[yy, :, at], ogs[...], over_tokens, preferred_element_type=F32)
+            tt[rows(yy, i), :] = t.astype(BF)
+            return 0
+
+        lax.fori_loop(0, 4, sub, 0)
 
     def add_into(dst, dst_row, *sources):
         def sub(i, _):
@@ -197,7 +193,9 @@
         lax.fori_loop(0, QR // 64, sub, 0)
 
     f_w.wait()
-    layer(me, 0)
+    for copy in f_act:
+        copy.wait()
+    layer(me)
 
     def core_sum(zz, h):
         def sub(i, _):
@@ -225,6 +223,13 @@
     core_sum(z, 0)
     core_sum(z, 1)
 
+    arrived(ogs, ("og",), "S")
+    term(0)
+    for q in (0, 2, 1, 3):
+        way = "D" if q < 2 else "U"
+        side = 1 if q < 2 else 0
+        send(tt.at[rows(yo, q)], rb.at[side, pl.ds((q % 2) * QR, QR)], ("rb", way, q % 2), way)
+
     for q in (0, 1):
         arrived(wg.at[rows(bd, q)], ("g1", "U", q), "D")
         send(wg.at[rows(bd, q)], wg.at[rows(bd, q)], ("g2", "U", q), "U")
@@ -234,7 +239,7 @@
         send(wg.at[rows(bu, q)], wg.at[rows(bu, q)], ("g2", "D", q), "D")
         arrived(wg.at[rows(bd, q)], ("g1", "U", q), "D")
 
-    def z_add(dst, h, zz, way):
+    def z_add(h, zz, way):
         def sub(i, _):
             at = pl.ds(pl.multiple_of(i * 128, 128), 128)
             for l in HS:
@@ -246,17 +251,15 @@
         lax.fori_loop(0, 4, sub, 0)
 
     arrived(zb.at[0], ("zb", "U"), "ZD")
-    z_add(sel, 1, zu, 0)
+    z_add(1, zu, 0)
     send(sel.at[c, 1, zu], zc.at[0, 1], ("zc", "U", 1), "ZU")
     arrived(zb.at[1], ("zb", "D"), "ZU")
-    z_add(sel, 0, zd, 1)
+    z_add(0, zd, 1)
     send(sel.at[c, 0, zd], zc.at[1, 0], ("zc", "D", 0), "ZD")
 
-    layer(bd, 1)
-    layer(bu, 2)
-    for q in QS:
-        arrived(wg.at[rows(sib, q)], ("g1", "S", q), "S")
-    layer(sib, 3)
+    term(1)
+    for q in (0, 1):
+        send(tt.at[rows(yu, q)], rc.at[0, pl.ds(q * QR, QR)], ("rc", "U", q), "U")
 
     for h in HS:
         arrived(zc.at[0, h], ("zc", "U", h), "ZD")
@@ -274,22 +277,22 @@
         lax.fori_loop(0, 4, z_sum, 0)
         send(sel.at[c, h, z, 1 - xl], xr.at[h], ("xr", h), "X")
 
-    for q in (0, 2, 1, 3):
-        arrived(rx1.at[pl.ds(q * QR, QR)], ("x1", q), "S")
-        add_into(tt, bo * BLK + q * QR, (rx1, q * QR))
-        way = "D" if q < 2 else "U"
-        side = 1 if q < 2 else 0
-        send(tt.at[rows(bo, q)], rb.at[side, pl.ds((q % 2) * QR, QR)], ("rb", way, q % 2), way)
-
-    for q in (0, 1):
-        for w in "UD":
-            send(wg.at[rows(sib, q)], wg.at[rows(sib, q)], ("g3", w, q), w)
-
-    for q in QS:
-        arrived(ra.at[0, pl.ds(q * QR, QR)], ("ra", "U", q), "D")
-        arrived(ra.at[1, pl.ds(q * QR, QR)], ("ra", "D", q), "U")
-        add_into(tt, sib * BLK + q * QR, (ra.at[0], q * QR), (ra.at[1], q * QR))
-        send(tt.at[rows(sib, q)], rx2.at[pl.ds(q * QR, QR)], ("x2", q), "S")
+    weight_to_sibling(0)
+    layer(bd)
+    layer(bu)
+
+    term(2)
+    for q in (2, 3):
+        send(tt.at[rows(yd, q)], rc.at[1, pl.ds(q * QR, QR)], ("rc", "D", q), "D")
+
+    for i in HS:
+        q = 2 + i
+        arrived(rb.at[0, pl.ds(i * QR, QR)], ("rb", "U", i), "D")
+        add_into(tt, yu * BLK + q * QR, (rb.at[0], i * QR))
+        send(tt.at[rows(yu, q)], rc.at[0, pl.ds(q * QR, QR)], ("rc", "U", q), "U")
+        arrived(rb.at[1, pl.ds(i * QR, QR)], ("rb", "D", i), "U")
+        add_into(tt, yd * BLK + i * QR, (rb.at[1], i * QR))
+        send(tt.at[rows(yd, i)], rc.at[1, pl.ds(i * QR, QR)], ("rc", "D", i), "D")
 
     f_mast.wait()
     f_mom.wait()
@@ -318,13 +321,24 @@
 
         lax.fori_loop(0, 8, update, 0)
         send(npv.at[c, h, z, xl], npv.at[c, h, z, xl], ("xp", h), "X")
-    out_copies.append(fetch(nm, nm_o, "nm"))
-    out_copies.append(fetch(nmo, nmo_o, "nmo"))
+
+    for q in (3, 1, 2):
+        weight_to_sibling(q)
+    tokens_to_sibling(3)
 
     for q in QS:
         way, back = ("U", "D") if q < 2 else ("D", "U")
         arrived(wg.at[rows(bo, q)], ("g2", way, q), back)
-        send(wg.at[rows(bo, q)], wg.at[rows(bo, q)], ("g4", q), "S")
+        if q in (1, 2):
+            send(wg.at[rows(bo, q)], wg.at[rows(bo, q)], ("g4", q), "S")
+    layer(bo)
+
+    def pass_on(q):
+        arrived(wg.at[rows(sib, q)], ("g1", "S", q), "S")
+        for w in "UD":
+            send(wg.at[rows(sib, q)], wg.at[rows(sib, q)], ("g3", w, q), w)
+
+    pass_on(0)
 
     for h in HS:
         arrived(npv.at[c, h, z, 1 - xl], ("xp", h), "X")
@@ -332,22 +346,8 @@
             send(npv.at[c, h, z], npv.at[c, h, z], ("zp", w, h), "Z" + w)
         send(npv.at[c, h, z], npv.at[c, h, z], ("c2", 0, h), "C")
 
-    layer(bo, 4)
-
-    for i in HS:
-        arrived(rb.at[0, pl.ds(i * QR, QR)], ("rb", "U", i), "D")
-        add_into(tt, bu * BLK + (2 + i) * QR, (rb.at[0], i * QR))
-        q = 2 + i
-        send(tt.at[rows(bu, q)], rc.at[0, pl.ds(q * QR, QR)], ("rc", "U", q), "U")
-        arrived(rb.at[1, pl.ds(i * QR, QR)], ("rb", "D", i), "U")
-        add_into(tt, bd * BLK + i * QR, (rb.at[1], i * QR))
-        send(tt.at[rows(bd, i)], rc.at[1, pl.ds(i * QR, QR)], ("rc", "D", i), "D")
-
-    for q in (2, 3):
-        for w in "UD":
-            send(wg.at[rows(sib, q)], wg.at[rows(sib, q)], ("g3", w, q), w)
-
     for h in HS:
+        pass_on((3, 1)[h])
         arrived(npv.at[c, h, zd], ("zp", "U", h), "ZD")
         if h == 0:
             send(npv.at[c, 0, zd], npv.at[c, 0, zd], ("zf", "U"), "ZU")
@@ -356,10 +356,35 @@
         if h == 1:
             send(npv.at[c, 1, zu], npv.at[c, 1, zu], ("zf", "D"), "ZD")
         send(npv.at[c, h, zu], npv.at[c, h, zu], ("c2", 2, h), "C")
+    pass_on(2)
+
+    arrived(wg.at[rows(bds, 0)], ("g3", "U", 0), "D")
+    send(wg.at[rows(bds, 0)], wg.at[rows(bds, 0)], ("g5", "U"), "U")
+    arrived(wg.at[rows(bus, 3)], ("g3", "D", 3), "U")
+    send(wg.at[rows(bus, 3)], wg.at[rows(bus, 3)], ("g5", "D"), "D")
+
     arrived(npv.at[c, 0, zo], ("zf", "U"), "ZD")
     send(npv.at[c, 0, zo], npv.at[c, 0, zo], ("c2", 3, 0), "C")
     arrived(npv.at[c, 1, zo], ("zf", "D"), "ZU")
     send(npv.at[c, 1, zo], npv.at[c, 1, zo], ("c2", 3, 1), "C")
+
+    layer(sib)
+
+    term(3)
+    for q in QS:
+        arrived(rc.at[0, pl.ds(q * QR, QR)], ("rc", "U", q), "D")
+        arrived(rc.at[1, pl.ds(q * QR, QR)], ("rc", "D", q), "U")
+
+        def grad_sum(i, _, q=q):
+            at = pl.ds(pl.multiple_of(q * QR + i * 64, 64), 64)
+            wg_o[0, at, :] = (
+                tt[pl.ds(pl.multiple_of(y * BLK + q * QR + i * 64, 64), 64), :].astype(F32)
+                + rc[0, at, :].astype(F32)
+                + rc[1, at, :].astype(F32)
+            ).astype(BF)
+            return 0
+
+        lax.fori_loop(0, 4, grad_sum, 0)
 
     for h in HS:
         for k, zz in enumerate((z, zd, zu, zo)):
@@ -372,47 +397,57 @@
                 ls.at[LSEM["np"]],
             ).start()
 
-    for q in QS:
+    layer(bds, 0, 1)
+    layer(bus, 3, 1)
+    arrived(wg.at[rows(bds, 3)], ("g3", "U", 3), "D")
+    layer(bds, 3, 1)
+    arrived(wg.at[rows(bus, 0)], ("g3", "D", 0), "U")
+    layer(bus, 0, 1)
+    for q in (1, 2):
         arrived(wg.at[rows(bos, q)], ("g4", q), "S")
-    layer(bos, 5)
-
-    for q in QS:
-        arrived(rx2.at[pl.ds(q * QR, QR)], ("x2", q), "S")
-    for q in QS:
-        arrived(rc.at[0, pl.ds(q * QR, QR)], ("rc", "U", q), "D")
-        arrived(rc.at[1, pl.ds(q * QR, QR)], ("rc", "D", q), "U")
-        add_into(tt, me * BLK + q * QR, (rc.at[0], q * QR), (rc.at[1], q * QR), (rx2, q * QR))
-    out_copies.append(fetch(tt.at[rows(me, 0, BLK)], wg_o.at[0], "wg"))
-
-    for n, (block, way, back) in enumerate(((bds, "U", "D"), (bus, "D", "U"))):
-        for q in QS:
-            arrived(wg.at[rows(block, q)], ("g3", way, q), back)
-        layer(block, 6 + n)
-    keysv[...] = acc[...].astype(BF)
-    out_copies.append(fetch(keysv, keys_o.at[0], "keys"))
+        arrived(wg.at[rows(bds, q)], ("g3", "U", q), "D")
+        arrived(wg.at[rows(bus, q)], ("g3", "D", q), "U")
+        for block in (bos, bds, bus):
+            layer(block, q, 1)
+    arrived(wg.at[rows(bos, 0)], ("g5", "U"), "D")
+    layer(bos, 0, 1)
+    arrived(wg.at[rows(bos, 3)], ("g5", "D"), "U")
+    layer(bos, 3, 1)
+    keys_o[0] = acc[...].astype(BF)
 
     for copy in started:
         copy.wait_send()
-    for copy in out_copies:
+    pltpu.make_async_copy(np_o, np_o, ls.at[LSEM["np"]]).wait()
+
+
+def write_out(*refs):
+    n = len(refs) // 2
+    sems = refs[-1]
+    copies = [pltpu.make_async_copy(refs[i], refs[n + i], sems.at[i]) for i in range(n)]
+    for copy in copies:
+        copy.start()
+    for copy in copies:
         copy.wait()
-    pltpu.make_async_copy(np_o, np_o, ls.at[LSEM["np"]]).wait()
 
 
 def body(plan, local_params, master, momentum, inner_weight, activations, out_grad):
     vm = pltpu.VMEM
     any_spec = pl.BlockSpec(memory_space=pl.ANY)
-    return pl.pallas_call(
+    vm_spec = pl.BlockSpec(memory_space=vm)
+    outs = (
+        ((BLK, KVC), BF),
+        ((BLK, 128), F32),
+        ((BLK, 128), F32),
+        ((1, TOK, INNER), BF),
+        ((1, TOK, D), BF),
+        ((1, BLK, INNER), BF),
+    )
+    given = (plan.reshape(8, 128), local_params, master, momentum, inner_weight, activations, out_grad)
+    results = pl.pallas_call(
         kernel,
-        out_shape=(
-            jax.ShapeDtypeStruct((BLK, KVC), BF),
-            jax.ShapeDtypeStruct((BLK, 128), F32),
-            jax.ShapeDtypeStruct((BLK, 128), F32),
-            jax.ShapeDtypeStruct((1, TOK, INNER), BF),
-            jax.ShapeDtypeStruct((1, TOK, D), BF),
-            jax.ShapeDtypeStruct((1, BLK, INNER), BF),
-        ),
+        out_shape=tuple(vm(*out) for out in outs),
         in_specs=[any_spec] * 7,
-        out_specs=[any_spec] * 6,
+        out_specs=[vm_spec] * 6,
         scratch_shapes=[
             vm((8, 128), jnp.int32),
             vm((BLK, 128), F32),
@@ -425,32 +460,36 @@
             vm((2, 2, 4, 2, HALF, 128), BF),
             vm((2, BLK, 128), F32),
             vm((2, BLK, 128), F32),
-            vm((BLK, 128), F32),
-            vm((BLK, 128), F32),
             vm((TOK, D), BF),
             vm((TOK, INNER), BF),
+            vm((4, TOK, BLK), BF),
+            vm((TOK, INNER), BF),
             vm((D, INNER), BF),
-            vm((D, INNER), BF),
-            vm((2, BLK, INNER), BF),
-            vm((BLK, INNER), BF),
+            vm((4 * BLK, INNER), BF),
             vm((2, HALF, INNER), BF),
             vm((2, BLK, INNER), BF),
-            vm((BLK, INNER), BF),
-            vm((TOK, D), BF),
             vm((TOK, INNER), F32),
-            vm((TOK, INNER), BF),
             pltpu.SemaphoreType.DMA((len(KEYS),)),
             pltpu.SemaphoreType.DMA((len(KEYS),)),
             pltpu.SemaphoreType.DMA((len(LOCAL),)),
         ],
         compiler_params=pltpu.CompilerParams(
-            collective_id=0, has_side_effects=True, vmem_limit_bytes=60 << 20
+            collective_id=0, has_side_effects=True, vmem_limit_bytes=44 << 20
         ),
         cost_estimate=pl.CostEstimate(
             flops=6 * TOK * D * INNER, bytes_accessed=26 << 20, transcendentals=0
         ),
         name="sync_and_layer",
-    )(plan.reshape(8, 128), local_params, master, momentum, inner_weight, activations, out_grad)
+    )(*(pltpu.with_memory_space_constraint(a, pltpu.HBM) for a in given))
+    return pl.pallas_call(
+        write_out,
+        out_shape=tuple(jax.ShapeDtypeStruct(*out) for out in outs),
+        in_specs=[vm_spec] * 6,
+        out_specs=[any_spec] * 6,
+        scratch_shapes=[pltpu.SemaphoreType.DMA((6,))],
+        compiler_params=pltpu.CompilerParams(vmem_limit_bytes=1 << 20),
+        name="write_out",
+    )(*(pltpu.with_memory_space_constraint(r, vm) for r in results))
 
 
 def solution(mesh):

time: 136 us -> 111 us (0.82)
  Pallas kernels: 125 us -> 110 us
  local copies, waits for them, and re-layouts: 10.2 us -> 0 us
    pallas_call x1 -> x2, Pallas kernels: 125 us -> 110 us  [the longest x1 106 us: body(): pl.pallas_call(kernel, out_shape=tuple((vm(*out) for out in outs)), in_sp...]
    unnamed x16 -> x0, local copies, waits for them, and re-layouts: 10.2 us -> none
where the time goes in v2:
time: 111 us
  Pallas kernels  110 us (99%)
    pallas_call x1, Pallas kernels, body(): pl.pallas_call(kernel, out_shape=tuple((vm(*out) for out in outs)), in_sp...  106 us
    pallas_call x1, Pallas kernels, body(): pl.pallas_call(write_out, out_shape=tuple((jax.ShapeDtypeStruct(*out) for...  4.06 us

profile of v2, /device:TPU:0, one launch (start us, length us, event | category | flops | bytes accessed | tf_op | source)
XLA Modules:
  0.0 111.1 jit_solution(685989541408715056)
XLA Ops:
  0.6 106.4 %sync_and_layer.1 = (bf16[1024,2048]{1,0:T(8,128)(2,1)S(1)}, f32[1024,128]{1,0:T(8,128)S(1)}, f32[1024,128]{1,0:T(8,128)S(1)}, bf16[1,256,512]{2,1,0:T(8,128)(2,...) custom-call(s32[8,128]{1,0:T(8,128)} %bitcast.1, bf16[2,1,1024,2048]{3,2,1,0:T(8,128)(2,1)} %lp_h.1, ...), custom_call_target="tpu_custom_call" | custom-call | flops 6442450944 | bytes 27262976 | tf_op jit(solution)/shard_map/sync_and_layer/pallas_call | solution.py:446
  107.0 4.1 %write_out.1 = (bf16[1024,2048]{1,0:T(8,128)(2,1)}, f32[1024,128]{1,0:T(8,128)}, f32[1024,128]{1,0:T(8,128)}, bf16[1,256,512]{2,1,0:T(8,128)(2,1)}, bf16[1,256,8...) custom-call(bf16[1024,2048]{1,0:T(8,128)(2,1)S(1)} %get-tuple-element.12.refs_0_, ...), custom_call_target="tpu_custom_call" | custom-call | tf_op jit(solution)/shard_map/write_out/pallas_call | solution.py:484

commit v3 on v2

--- a/solution.py
+++ b/solution.py
@@ -49,7 +49,7 @@
     np_o, nm, nmo, keys_o, ig, wg_o,
     plan_v, pick, lpb, sel, cr, zb, zc, xr, npv, mast, mom,
     act, og, acts, ogs, wg, tt, rb, rc, acc,
-    ss, rs, ls,
+    ss, rs, ls, here,
 ):
     rep, shard = lax.axis_index("rep"), lax.axis_index("shard")
     z, xl, c = rep // 4, (rep // 2) % 2, rep % 2
@@ -91,6 +91,38 @@
     def cols(block, i=0, n=BLK):
         return pl.ds(pl.multiple_of(block * BLK + i, QR), n)
 
+    barrier = pltpu.get_barrier_semaphore()
+
+    def signal(semaphore, way):
+        pl.semaphore_signal(semaphore, inc=1, device_id=to[way], device_id_type=pl.DeviceIdType.MESH)
+
+    for way in ("U", "D", "S", "X", "C"):
+        signal(barrier, way)
+    pl.when(z < 3)(lambda: signal(barrier, "ZU"))
+    pl.when(z == 0)(lambda: signal(barrier, "ZD"))
+    pl.semaphore_wait(barrier, 5 + jnp.where(z == 0, 0, jnp.where(z == 3, 2, 1)))
+    pl.when(z > 0)(lambda: signal(here, "ZD"))
+    pl.when(z == 3)(lambda: signal(here, "ZU"))
+
+    def tokens_to_sibling(k):
+        yy = (yo, yu, yd, y)[k]
+        send(act_h.at[0, :, cols(yy * 2 + 1 - xh)], acts.at[yy], ("ax", k), "S")
+
+    def weight_to(w, q):
+        send(w_h.at[0, pl.ds(q * QR, QR)], wg.at[rows(me, q)], ("g1", w, q), w)
+
+    def weight_to_sibling(q):
+        weight_to("S", q)
+
+    for q in QS:
+        weight_to("U", q)
+        weight_to("D", 3 - q)
+        if q == 0:
+            send(og_h.at[0], ogs, ("og",), "S")
+            tokens_to_sibling(0)
+    tokens_to_sibling(1)
+    tokens_to_sibling(2)
+
     f_plan = fetch(plan_h, plan_v, "plan")
     f_lp = [
         fetch(lp_h.at[:, 0, pl.ds(k * QR, QR)], lpb.at[k % 2], ("lp", k)) for k in (0, 1)
@@ -102,25 +134,6 @@
     f_mast = fetch(mast_h, mast, "mast")
     f_mom = fetch(mom_h, mom, "mom")
 
-    barrier = pltpu.get_barrier_semaphore()
-    for device in to.values():
-        pl.semaphore_signal(barrier, inc=1, device_id=device, device_id_type=pl.DeviceIdType.MESH)
-    pl.semaphore_wait(barrier, len(to))
-
-    def tokens_to_sibling(k):
-        yy = (yo, yu, yd, y)[k]
-        send(act_h.at[0, :, cols(yy * 2 + 1 - xh)], acts.at[yy], ("ax", k), "S")
-
-    for q in QS:
-        for w in "UD":
-            send(w_h.at[0, pl.ds(q * QR, QR)], wg.at[rows(me, q)], ("g1", w, q), w)
-        if q == 0:
-            send(og_h.at[0], ogs, ("og",), "S")
-            tokens_to_sibling(0)
-    tokens_to_sibling(1)
-
-    def weight_to_sibling(q):
-        send(w_h.at[0, pl.ds(q * QR, QR)], wg.at[rows(me, q)], ("g1", "S", q), "S")
 
     f_plan.wait()
     for g in range(8):
@@ -168,7 +181,7 @@
         yy = (yo, yu, yd, y)[k]
         arrived(acts.at[yy], ("ax", k), "S")
         if k == 0:
-            tokens_to_sibling(2)
+            weight_to_sibling(0)
 
         def sub(i, _):
             at = pl.ds(pl.multiple_of(i * QR, QR), QR)
@@ -211,6 +224,7 @@
     for h in HS:
         arrived(cr.at[h], ("c1", h), "C")
     core_sum(zo, 0)
+    pl.when(z < 3)(lambda: pl.semaphore_wait(here, jnp.where(z == 0, 2, 1)))
     send(sel.at[c, 0, zo], zb.at[1], ("zb", "D"), "ZD")
     core_sum(zo, 1)
     send(sel.at[c, 1, zo], zb.at[0], ("zb", "U"), "ZU")
@@ -223,21 +237,18 @@
     core_sum(z, 0)
     core_sum(z, 1)
 
+    for q in (0, 1):
+        arrived(wg.at[rows(bd, q)], ("g1", "U", q), "D")
+        send(wg.at[rows(bd, q)], wg.at[rows(bd, q)], ("g2", "U", q), "U")
+        arrived(wg.at[rows(bu, 3 - q)], ("g1", "D", 3 - q), "U")
+        send(wg.at[rows(bu, 3 - q)], wg.at[rows(bu, 3 - q)], ("g2", "D", 3 - q), "D")
+
     arrived(ogs, ("og",), "S")
     term(0)
     for q in (0, 2, 1, 3):
         way = "D" if q < 2 else "U"
         side = 1 if q < 2 else 0
         send(tt.at[rows(yo, q)], rb.at[side, pl.ds((q % 2) * QR, QR)], ("rb", way, q % 2), way)
-
-    for q in (0, 1):
-        arrived(wg.at[rows(bd, q)], ("g1", "U", q), "D")
-        send(wg.at[rows(bd, q)], wg.at[rows(bd, q)], ("g2", "U", q), "U")
-        arrived(wg.at[rows(bu, q)], ("g1", "D", q), "U")
-    for q in (2, 3):
-        arrived(wg.at[rows(bu, q)], ("g1", "D", q), "U")
-        send(wg.at[rows(bu, q)], wg.at[rows(bu, q)], ("g2", "D", q), "D")
-        arrived(wg.at[rows(bd, q)], ("g1", "U", q), "D")
 
     def z_add(h, zz, way):
         def sub(i, _):
@@ -277,7 +288,10 @@
         lax.fori_loop(0, 4, z_sum, 0)
         send(sel.at[c, h, z, 1 - xl], xr.at[h], ("xr", h), "X")
 
-    weight_to_sibling(0)
+    weight_to_sibling(3)
+    for q in (2, 3):
+        arrived(wg.at[rows(bd, q)], ("g1", "U", q), "D")
+        arrived(wg.at[rows(bu, 3 - q)], ("g1", "D", 3 - q), "U")
     layer(bd)
     layer(bu)
 
@@ -322,7 +336,7 @@
         lax.fori_loop(0, 8, update, 0)
         send(npv.at[c, h, z, xl], npv.at[c, h, z, xl], ("xp", h), "X")
 
-    for q in (3, 1, 2):
+    for q in (1, 2):
         weight_to_sibling(q)
     tokens_to_sibling(3)
 
@@ -403,21 +417,24 @@
     layer(bds, 3, 1)
     arrived(wg.at[rows(bus, 0)], ("g3", "D", 0), "U")
     layer(bus, 0, 1)
+    pltpu.make_async_copy(np_o, np_o, ls.at[LSEM["np"]]).wait()
+    last = 16
     for q in (1, 2):
         arrived(wg.at[rows(bos, q)], ("g4", q), "S")
         arrived(wg.at[rows(bds, q)], ("g3", "U", q), "D")
         arrived(wg.at[rows(bus, q)], ("g3", "D", q), "U")
         for block in (bos, bds, bus):
             layer(block, q, 1)
+        if q == 1:
+            for copy in started[:-last]:
+                copy.wait_send()
     arrived(wg.at[rows(bos, 0)], ("g5", "U"), "D")
     layer(bos, 0, 1)
     arrived(wg.at[rows(bos, 3)], ("g5", "D"), "U")
     layer(bos, 3, 1)
     keys_o[0] = acc[...].astype(BF)
-
-    for copy in started:
+    for copy in started[-last:]:
         copy.wait_send()
-    pltpu.make_async_copy(np_o, np_o, ls.at[LSEM["np"]]).wait()
 
 
 def write_out(*refs):
@@ -472,6 +489,7 @@
             pltpu.SemaphoreType.DMA((len(KEYS),)),
             pltpu.SemaphoreType.DMA((len(KEYS),)),
             pltpu.SemaphoreType.DMA((len(LOCAL),)),
+            pltpu.SemaphoreType.REGULAR,
         ],
         compiler_params=pltpu.CompilerParams(
             collective_id=0, has_side_effects=True, vmem_limit_bytes=44 << 20

time: 111 us -> 110 us (level)
    pallas_call x1, Pallas kernels: 106 us -> 105 us  [body(): pl.pallas_call(kernel, out_shape=tuple((vm(*out) for out in outs)), in_sp...]
where the time goes in v3:
time: 110 us
  Pallas kernels  109 us (99%)
    pallas_call x1, Pallas kernels, body(): pl.pallas_call(kernel, out_shape=tuple((vm(*out) for out in outs)), in_sp...  105 us
    pallas_call x1, Pallas kernels, body(): pl.pallas_call(write_out, out_shape=tuple((jax.ShapeDtypeStruct(*out) for...  4.06 us

profile of v3, /device:TPU:0, one launch (start us, length us, event | category | flops | bytes accessed | tf_op | source)
XLA Modules:
  0.0 109.9 jit_solution(15448437885341189337)
XLA Ops:
  0.6 105.2 %sync_and_layer.1 = (bf16[1024,2048]{1,0:T(8,128)(2,1)S(1)}, f32[1024,128]{1,0:T(8,128)S(1)}, f32[1024,128]{1,0:T(8,128)S(1)}, bf16[1,256,512]{2,1,0:T(8,128)(2,...) custom-call(s32[8,128]{1,0:T(8,128)} %bitcast.1, bf16[2,1,1024,2048]{3,2,1,0:T(8,128)(2,1)} %lp_h.1, ...), custom_call_target="tpu_custom_call" | custom-call | flops 6442450944 | bytes 27262976 | tf_op jit(solution)/shard_map/sync_and_layer/pallas_call | solution.py:463
  105.9 4.1 %write_out.1 = (bf16[1024,2048]{1,0:T(8,128)(2,1)}, f32[1024,128]{1,0:T(8,128)}, f32[1024,128]{1,0:T(8,128)}, bf16[1,256,512]{2,1,0:T(8,128)(2,1)}, bf16[1,256,8...) custom-call(bf16[1024,2048]{1,0:T(8,128)(2,1)S(1)} %get-tuple-element.12.refs_0_, ...), custom_call_target="tpu_custom_call" | custom-call | tf_op jit(solution)/shard_map/write_out/pallas_call | solution.py:502

commit v4 on v3

--- a/solution.py
+++ b/solution.py
@@ -36,6 +36,7 @@
     + [("c2", k, h) for k in range(4) for h in HS]
 )
 SEM = {key: i for i, key in enumerate(KEYS)}
+LATE = (("g4", 2), ("g5", "U"), ("g5", "D"), ("g3", "U", 2), ("g3", "D", 2))
 LOCAL = (
     ["og", "plan", "w", "mast", "mom", "np"]
     + [("act", j) for j in range(8)]
@@ -64,21 +65,20 @@
         "X": (z * 4 + (1 - xl) * 2 + c, shard), "C": (z * 4 + xl * 2 + 1 - c, shard),
         "ZU": (zu * 4 + xl * 2 + c, shard), "ZD": (zd * 4 + xl * 2 + c, shard),
     }
-    started = []
-
-    def send(src, dst, key, way):
-        copy = pltpu.make_async_remote_copy(
+    started, late = [], []
+
+    def remote(src, dst, key, way):
+        return pltpu.make_async_remote_copy(
             src_ref=src, dst_ref=dst, send_sem=ss.at[SEM[key]], recv_sem=rs.at[SEM[key]],
             device_id=to[way], device_id_type=pl.DeviceIdType.MESH,
         )
-        copy.start()
-        started.append(copy)
+
+    def send(src, dst, key, way):
+        remote(src, dst, key, way).start()
+        (late if key in LATE else started).append((src, dst, key, way))
 
     def arrived(dst, key, way):
-        pltpu.make_async_remote_copy(
-            src_ref=dst, dst_ref=dst, send_sem=ss.at[SEM[key]], recv_sem=rs.at[SEM[key]],
-            device_id=to[way], device_id_type=pl.DeviceIdType.MESH,
-        ).wait_recv()
+        remote(dst, dst, key, way).wait_recv()
 
     def fetch(src, dst, key):
         copy = pltpu.make_async_copy(src, dst, ls.at[LSEM[key]])
@@ -96,32 +96,56 @@
     def signal(semaphore, way):
         pl.semaphore_signal(semaphore, inc=1, device_id=to[way], device_id_type=pl.DeviceIdType.MESH)
 
-    for way in ("U", "D", "S", "X", "C"):
-        signal(barrier, way)
-    pl.when(z < 3)(lambda: signal(barrier, "ZU"))
-    pl.when(z == 0)(lambda: signal(barrier, "ZD"))
-    pl.semaphore_wait(barrier, 5 + jnp.where(z == 0, 0, jnp.where(z == 3, 2, 1)))
-    pl.when(z > 0)(lambda: signal(here, "ZD"))
-    pl.when(z == 3)(lambda: signal(here, "ZU"))
+    before = {
+        "U": y == 3, "D": y > 0, "S": xh == 1, "X": xl == 1, "ZU": z == 3, "ZD": z > 0,
+    }
+    back_of = {"U": "D", "D": "U", "S": "S", "X": "X", "ZU": "ZD", "ZD": "ZU"}
+    slot = {way: i for i, way in enumerate(before)}
+    signal(barrier, "C")
+    for way, first in before.items():
+        pl.when(jnp.logical_not(first))(lambda way=way: signal(barrier, way))
+    expected = 1
+    for first in before.values():
+        expected = expected + jnp.where(first, 1, 0)
+    pl.semaphore_wait(barrier, expected)
+    for way, first in before.items():
+        pl.when(first)(lambda way=way: signal(here.at[slot[back_of[way]]], way))
+
+    def answered(way):
+        pl.when(jnp.logical_not(before[way]))(lambda: pl.semaphore_wait(here.at[slot[way]], 1))
+
+    def tokens(k):
+        yy = (yo, yu, yd, y)[k]
+        return act_h.at[0, :, cols(yy * 2 + 1 - xh)], acts.at[yy], ("ax", k), "S"
+
+    def weight(w, q):
+        return w_h.at[0, pl.ds(q * QR, QR)], wg.at[rows(me, q)], ("g1", w, q), w
 
     def tokens_to_sibling(k):
-        yy = (yo, yu, yd, y)[k]
-        send(act_h.at[0, :, cols(yy * 2 + 1 - xh)], acts.at[yy], ("ax", k), "S")
-
-    def weight_to(w, q):
-        send(w_h.at[0, pl.ds(q * QR, QR)], wg.at[rows(me, q)], ("g1", w, q), w)
+        send(*tokens(k))
 
     def weight_to_sibling(q):
-        weight_to("S", q)
-
-    for q in QS:
-        weight_to("U", q)
-        weight_to("D", 3 - q)
-        if q == 0:
-            send(og_h.at[0], ogs, ("og",), "S")
-            tokens_to_sibling(0)
-    tokens_to_sibling(1)
-    tokens_to_sibling(2)
+        send(*weight("S", q))
+
+    def first_copies(way):
+        if way == "S":
+            return [(og_h.at[0], ogs, ("og",), "S")] + [tokens(k) for k in range(3)]
+        return [weight(way, q) for q in ((0, 1, 2, 3) if way == "U" else (3, 2, 1, 0))]
+
+    def first_sends(way):
+        for copy in first_copies(way):
+            remote(*copy).start()
+
+    for way in ("U", "D", "S"):
+        pl.when(before[way])(lambda way=way: first_sends(way))
+    for way in ("U", "S", "D"):
+
+        @pl.when(jnp.logical_not(before[way]))
+        def _(way=way):
+            pl.semaphore_wait(here.at[slot[way]], 1)
+            first_sends(way)
+
+        started.extend(first_copies(way))
 
     f_plan = fetch(plan_h, plan_v, "plan")
     f_lp = [
@@ -224,7 +248,8 @@
     for h in HS:
         arrived(cr.at[h], ("c1", h), "C")
     core_sum(zo, 0)
-    pl.when(z < 3)(lambda: pl.semaphore_wait(here, jnp.where(z == 0, 2, 1)))
+    answered("ZU")
+    answered("ZD")
     send(sel.at[c, 0, zo], zb.at[1], ("zb", "D"), "ZD")
     core_sum(zo, 1)
     send(sel.at[c, 1, zo], zb.at[0], ("zb", "U"), "ZU")
@@ -272,6 +297,7 @@
     for q in (0, 1):
         send(tt.at[rows(yu, q)], rc.at[0, pl.ds(q * QR, QR)], ("rc", "U", q), "U")
 
+    answered("X")
     for h in HS:
         arrived(zc.at[0, h], ("zc", "U", h), "ZD")
         arrived(zc.at[1, h], ("zc", "D", h), "ZU")
@@ -418,23 +444,24 @@
     arrived(wg.at[rows(bus, 0)], ("g3", "D", 0), "U")
     layer(bus, 0, 1)
     pltpu.make_async_copy(np_o, np_o, ls.at[LSEM["np"]]).wait()
-    last = 16
     for q in (1, 2):
-        arrived(wg.at[rows(bos, q)], ("g4", q), "S")
         arrived(wg.at[rows(bds, q)], ("g3", "U", q), "D")
+        layer(bds, q, 1)
         arrived(wg.at[rows(bus, q)], ("g3", "D", q), "U")
-        for block in (bos, bds, bus):
-            layer(block, q, 1)
-        if q == 1:
-            for copy in started[:-last]:
-                copy.wait_send()
+        layer(bus, q, 1)
+    arrived(wg.at[rows(bos, 1)], ("g4", 1), "S")
+    layer(bos, 1, 1)
+    for copy in started:
+        remote(*copy).wait_send()
     arrived(wg.at[rows(bos, 0)], ("g5", "U"), "D")
     layer(bos, 0, 1)
     arrived(wg.at[rows(bos, 3)], ("g5", "D"), "U")
     layer(bos, 3, 1)
+    arrived(wg.at[rows(bos, 2)], ("g4", 2), "S")
+    layer(bos, 2, 1)
     keys_o[0] = acc[...].astype(BF)
-    for copy in started[-last:]:
-        copy.wait_send()
+    for copy in late:
+        remote(*copy).wait_send()
 
 
 def write_out(*refs):
@@ -489,7 +516,7 @@
             pltpu.SemaphoreType.DMA((len(KEYS),)),
             pltpu.SemaphoreType.DMA((len(KEYS),)),
             pltpu.SemaphoreType.DMA((len(LOCAL),)),
-            pltpu.SemaphoreType.REGULAR,
+            pltpu.SemaphoreType.REGULAR((6,)),
         ],
         compiler_params=pltpu.CompilerParams(
             collective_id=0, has_side_effects=True, vmem_limit_bytes=44 << 20

time: 110 us -> 108 us (0.982)
  Pallas kernels: 109 us -> 107 us
    pallas_call x1, Pallas kernels: 105 us -> 103 us  [body(): pl.pallas_call(kernel, out_shape=tuple((vm(*out) for out in outs)), in_sp...]
where the time goes in v4:
time: 108 us
  Pallas kernels  107 us (99%)
    pallas_call x1, Pallas kernels, body(): pl.pallas_call(kernel, out_shape=tuple((vm(*out) for out in outs)), in_sp...  103 us
    pallas_call x1, Pallas kernels, body(): pl.pallas_call(write_out, out_shape=tuple((jax.ShapeDtypeStruct(*out) for...  4.06 us

profile of v4, /device:TPU:0, one launch (start us, length us, event | category | flops | bytes accessed | tf_op | source)
XLA Modules:
  0.0 107.6 jit_solution(488525093377122014)
XLA Ops:
  0.6 102.9 %sync_and_layer.1 = (bf16[1024,2048]{1,0:T(8,128)(2,1)S(1)}, f32[1024,128]{1,0:T(8,128)S(1)}, f32[1024,128]{1,0:T(8,128)S(1)}, bf16[1,256,512]{2,1,0:T(8,128)(2,...) custom-call(s32[8,128]{1,0:T(8,128)} %bitcast.1, bf16[2,1,1024,2048]{3,2,1,0:T(8,128)(2,1)} %lp_h.1, ...), custom_call_target="tpu_custom_call" | custom-call | flops 6442450944 | bytes 27262976 | tf_op jit(solution)/shard_map/sync_and_layer/pallas_call | solution.py:490
  103.5 4.1 %write_out.1 = (bf16[1024,2048]{1,0:T(8,128)(2,1)}, f32[1024,128]{1,0:T(8,128)}, f32[1024,128]{1,0:T(8,128)}, bf16[1,256,512]{2,1,0:T(8,128)(2,1)}, bf16[1,256,8...) custom-call(bf16[1024,2048]{1,0:T(8,128)(2,1)S(1)} %get-tuple-element.12.refs_0_, ...), custom_call_target="tpu_custom_call" | custom-call | tf_op jit(solution)/shard_map/write_out/pallas_call | solution.py:529

commit v5 on v4

--- a/solution.py
+++ b/solution.py
@@ -201,7 +201,7 @@
 
         lax.fori_loop(0, n, sub, 0)
 
-    def term(k):
+    def term(k, each=None):
         yy = (yo, yu, yd, y)[k]
         arrived(acts.at[yy], ("ax", k), "S")
         if k == 0:
@@ -216,7 +216,12 @@
             tt[rows(yy, i), :] = t.astype(BF)
             return 0
 
-        lax.fori_loop(0, 4, sub, 0)
+        if each is None:
+            lax.fori_loop(0, 4, sub, 0)
+        else:
+            for q in (0, 2, 1, 3):
+                lax.fori_loop(q, q + 1, sub, 0)
+                each(q)
 
     def add_into(dst, dst_row, *sources):
         def sub(i, _):
@@ -269,11 +274,12 @@
         send(wg.at[rows(bu, 3 - q)], wg.at[rows(bu, 3 - q)], ("g2", "D", 3 - q), "D")
 
     arrived(ogs, ("og",), "S")
-    term(0)
-    for q in (0, 2, 1, 3):
+    def far_block(q):
         way = "D" if q < 2 else "U"
         side = 1 if q < 2 else 0
         send(tt.at[rows(yo, q)], rb.at[side, pl.ds((q % 2) * QR, QR)], ("rb", way, q % 2), way)
+
+    term(0, far_block)
 
     def z_add(h, zz, way):
         def sub(i, _):

time: 108 us -> 108 us (level)
  no operation moved by 1% of the time
where the time goes in v5:
time: 108 us
  Pallas kernels  107 us (99%)
    pallas_call x1, Pallas kernels, body(): pl.pallas_call(kernel, out_shape=tuple((vm(*out) for out in outs)), in_sp...  103 us
    pallas_call x1, Pallas kernels, body(): pl.pallas_call(write_out, out_shape=tuple((jax.ShapeDtypeStruct(*out) for...  4.06 us

profile of v5, /device:TPU:0, one launch (start us, length us, event | category | flops | bytes accessed | tf_op | source)
XLA Modules:
  0.0 107.6 jit_solution(10361244299399994239)
XLA Ops:
  0.6 102.9 %sync_and_layer.1 = (bf16[1024,2048]{1,0:T(8,128)(2,1)S(1)}, f32[1024,128]{1,0:T(8,128)S(1)}, f32[1024,128]{1,0:T(8,128)S(1)}, bf16[1,256,512]{2,1,0:T(8,128)(2,...) custom-call(s32[8,128]{1,0:T(8,128)} %bitcast.1, bf16[2,1,1024,2048]{3,2,1,0:T(8,128)(2,1)} %lp_h.1, ...), custom_call_target="tpu_custom_call" | custom-call | flops 6442450944 | bytes 27262976 | tf_op jit(solution)/shard_map/sync_and_layer/pallas_call | solution.py:496
  103.5 4.1 %write_out.1 = (bf16[1024,2048]{1,0:T(8,128)(2,1)}, f32[1024,128]{1,0:T(8,128)}, f32[1024,128]{1,0:T(8,128)}, bf16[1,256,512]{2,1,0:T(8,128)(2,1)}, bf16[1,256,8...) custom-call(bf16[1024,2048]{1,0:T(8,128)(2,1)S(1)} %get-tuple-element.12.refs_0_, ...), custom_call_target="tpu_custom_call" | custom-call | tf_op jit(solution)/shard_map/write_out/pallas_call | solution.py:535
